TPU v7x, 256 devices: a whole 4x4x8 slice. The times are simulated.
256 devices in a mesh: bricks: 64 (over y, z, core), slab: 4 (over x).
Axes of the slice: x: 4, y: 4, z: 8, core: 2. Of those that a mesh axis runs over, the one named last changes fastest.
Arguments:
- part_pos: float32 [256, 3, 2048], P(('bricks', 'slab')), may hold values from 0 to 1, as said below
- part_mass: float32 [256, 2048], P(('bricks', 'slab')), may hold values from 0.5 to 2
- cell_pos: float32 [256, 3, 2048], P(('bricks', 'slab')), may hold values from 0 to 1, as said below
- cell_mass: float32 [256, 2048], P(('bricks', 'slab')), may hold values from 0.5 to 2
- cell_scale: float32 [256, 2048], P(('bricks', 'slab')), may hold values from 0.5 to 2
- req_tile: int32 [16384, 1], P(('bricks', 'slab')), may hold values from 0 to 15, as said below
- tile_bucket: int32 [256, 144], P(('bricks', 'slab')), may hold values from 0 to 15, as said below
- tile_slot: int32 [256, 144], P(('bricks', 'slab')), may hold values from 0 to 63, as said below
- tile_count: int32 [256], P(('bricks', 'slab')), may hold values from 64 to 144, as said below
- lagr_index: int32 [256, 2048], P(('bricks', 'slab')), may hold values from 0 to 2047, each once within a row
Outputs:
- particle_potential: float32 [256, 2048], P(('bricks', 'slab'))
- cell_potential: float32 [256, 2048], P(('bricks', 'slab'))
- divergence: float32 [16, 256, 128], P('slab', 'bricks')
Inputs may be any that keep to these rules, and one draw needn't show every extreme that they name: `part_pos`: device b * 4 + s holds particles of its own brick: component 0 within [0.25 b / 64, 0.25 (b + 1) / 64], component 1 within [0.25 s / 4, 0.25 (s + 1) / 4], component 2 within [0, 1]. `cell_pos`: device b * 4 + s holds the cells of the same brick, bounded as its particles. `req_tile`: over the devices of one slab index, every cell tile of every device is named by exactly four slots. `tile_bucket`: A device's live tiles name each of its buckets at least once. `tile_slot`: A device's live tiles name each of its slots at least once. `tile_count`: the live tiles are the first entries of a device's list; one device has exactly 144, every other between 64 and 80. `lagr_index`: each device's particles fill its block of the Lagrangian grid, one point each.
All inputs are finite; a program needn't handle non-finite values.
Results may differ from a plain program's by a relative error of at most 0.0003.
Values sent between devices are 32-bit elements; how exact they have to be, the bound alone decides.
A program may use at most 64 MiB of HBM per device.

v0:
```python
import jax
import jax.numpy as jnp
from jax import lax
from jax.sharding import PartitionSpec as P

TS = 128
ITERS = 2
LB = 4
EPS = 0.05
tile_group = 16


def with_halo(block, sides, width):
    for axis, dim in sides:
        count = lax.axis_size(axis)
        forward = [(i, i + 1) for i in range(count - 1)]
        backward = [(target, source) for source, target in forward]
        low = lax.ppermute(
            lax.slice_in_dim(block, block.shape[dim] - width, None, axis=dim), axis, forward
        )
        high = lax.ppermute(lax.slice_in_dim(block, 0, width, axis=dim), axis, backward)
        block = jnp.concatenate([low, block, high], axis=dim)
    return block


def tile_kernel(part_tiles, cell_tiles, live_mask):
    distance = (part_tiles[:, 0, :, None] - cell_tiles[:, 0, None, :]) ** 2
    distance = distance + (part_tiles[:, 1, :, None] - cell_tiles[:, 1, None, :]) ** 2
    distance = distance + (part_tiles[:, 2, :, None] - cell_tiles[:, 2, None, :]) ** 2
    return jnp.exp(-distance / EPS) * live_mask[:, None, None]


def grouped(arrays):
    return tuple(
        (
            item.reshape((item.shape[0] // tile_group, tile_group) + item.shape[1:])
            for item in arrays
        )
    )


def row_pass(part_rows, cell_rows, live_mask, buckets, value_rows, bucket_count):

    def row_one_group(pieces):
        part_piece, cell_piece, mask_piece, value_piece = pieces
        kernel = tile_kernel(part_piece, cell_piece, mask_piece)
        return jnp.einsum("tij,tcj->tci", kernel, value_piece, precision=lax.Precision.HIGHEST)

    per_tile = lax.map(row_one_group, grouped((part_rows, cell_rows, live_mask, value_rows)))
    per_tile = per_tile.reshape((-1,) + per_tile.shape[2:])
    one_hot = (buckets[:, None] == jnp.arange(bucket_count, dtype=jnp.int32)[None, :]).astype(
        jnp.float32
    )
    return jnp.einsum("tb,tci->bci", one_hot, per_tile, precision=lax.Precision.HIGHEST)


def column_pass(part_rows, cell_rows, live_mask, slot_ids, scale_rows, slot_total):

    def column_one_group(pieces):
        part_piece, cell_piece, mask_piece, scale_piece = pieces
        kernel = tile_kernel(part_piece, cell_piece, mask_piece)
        return jnp.einsum("tij,ti->tj", kernel, scale_piece, precision=lax.Precision.HIGHEST)

    per_tile = lax.map(column_one_group, grouped((part_rows, cell_rows, live_mask, scale_rows)))
    per_tile = per_tile.reshape((-1,) + per_tile.shape[2:])
    one_hot = (slot_ids[:, None] == jnp.arange(slot_total, dtype=jnp.int32)[None, :]).astype(
        jnp.float32
    )
    return jnp.einsum("ts,tj->sj", one_hot, per_tile, precision=lax.Precision.HIGHEST)


def on_device(
    part_pos,
    part_mass,
    cell_pos,
    cell_mass,
    cell_scale,
    req_tile,
    tile_bucket,
    tile_slot,
    tile_count,
    lagr_index,
):
    places = part_pos[0]
    tile_width = TS
    bucket_count = places.shape[1] // tile_width
    cell_tiles = cell_pos.shape[2] // tile_width
    brick_count = lax.axis_size("bricks")
    per_peer = req_tile.shape[1]
    slot_total = brick_count * per_peer
    part_tiles = places.reshape(3, bucket_count, tile_width).transpose(1, 0, 2)
    own_cells = cell_pos[0].reshape(3, cell_tiles, tile_width).transpose(1, 0, 2)
    buckets = tile_bucket[0]
    slot_ids = tile_slot[0]
    live_mask = (jnp.arange(buckets.shape[0], dtype=jnp.int32) < tile_count[0]).astype(jnp.float32)
    cell_ids = jnp.arange(cell_tiles, dtype=jnp.int32)
    wanted = (jnp.arange(brick_count, dtype=jnp.int32)[:, None] * cell_tiles + req_tile).reshape(
        slot_total
    )
    every_cell = lax.all_gather(own_cells, "bricks", axis=0, tiled=True)
    slot_cells = every_cell[wanted]

    def fetch_duals(values):
        return lax.all_gather(values, "bricks", axis=0, tiled=True)[wanted]

    part_rows = part_tiles[buckets]
    cell_rows = slot_cells[slot_ids]
    masses = part_mass[0].reshape(bucket_count, tile_width)
    cell_masses = cell_mass[0].reshape(cell_tiles, tile_width)
    cell_scaling = cell_scale[0].reshape(cell_tiles, tile_width)
    for sweep in range(ITERS):
        fetched = fetch_duals(cell_scaling[:, None, :])
        totals = row_pass(part_rows, cell_rows, live_mask, buckets, fetched[slot_ids], bucket_count)
        particle_scale = masses / totals[:, 0]
        partial_value = column_pass(
            part_rows, cell_rows, live_mask, slot_ids, particle_scale[buckets], slot_total
        )
        one_hot = (req_tile[:, :, None] == cell_ids[None, None, :]).astype(jnp.float32)
        dense_sums = jnp.einsum(
            "pcq,pct->pqt",
            one_hot,
            partial_value.reshape(brick_count, per_peer, tile_width),
            precision=lax.Precision.HIGHEST,
        )
        cell_scaling = cell_masses / lax.psum_scatter(
            dense_sums.reshape(brick_count * cell_tiles, tile_width),
            "bricks",
            scatter_dimension=0,
            tiled=True,
        )
    weighted = jnp.concatenate(
        [cell_scaling[:, None, :], cell_scaling[:, None, :] * own_cells], axis=1
    )
    fetched = fetch_duals(weighted)
    totals = row_pass(part_rows, cell_rows, live_mask, buckets, fetched[slot_ids], bucket_count)
    particle_scale = masses / totals[:, 0]
    displacement = totals[:, 1:] / totals[:, 0:1] - part_tiles
    displacement = displacement.transpose(1, 0, 2).reshape(3, bucket_count * tile_width)
    lagr_grid = jnp.zeros_like(displacement).at[:, lagr_index[0]].set(displacement)
    planes = lagr_grid.reshape(3, -1, LB, tile_width)
    across = with_halo(planes[0], (("slab", 0),), 1)
    second = with_halo(planes[1], (("bricks", 1),), 1)
    depth_pad = jnp.pad(planes[2], ((0, 0), (0, 0), (1, 1)))
    divergence = 0.5 * (across[2:] - across[:-2])
    divergence = divergence + 0.5 * (second[:, 2:] - second[:, :-2])
    divergence = divergence + 0.5 * (depth_pad[:, :, 2:] - depth_pad[:, :, :-2])
    particle_potential = jnp.log(particle_scale).reshape(1, -1)
    cell_potential = jnp.log(cell_scaling).reshape(1, -1)
    return (particle_potential, cell_potential, divergence)


def solution(mesh):
    return jax.shard_map(
        on_device,
        mesh=mesh,
        in_specs=(
            P(("bricks", "slab"), None, None),
            P(("bricks", "slab"), None),
            P(("bricks", "slab"), None, None),
            P(("bricks", "slab"), None),
            P(("bricks", "slab"), None),
            P(("bricks", "slab"), None),
            P(("bricks", "slab"), None),
            P(("bricks", "slab"), None),
            P(("bricks", "slab")),
            P(("bricks", "slab"), None),
        ),
        out_specs=(
            P(("bricks", "slab"), None),
            P(("bricks", "slab"), None),
            P("slab", "bricks", None),
        ),
        check_vma=False,
    )
```

profile of v0, /device:TPU:14, one launch (start us, length us, event | category | flops | bytes accessed | tf_op | source)
XLA Modules:
  0.0 641.0 jit_solution(7654722147235039259)
XLA Ops:
  11.5 53.0 %all_gather.13 = f32[1024,1,128]{2,0,1:T(8,128)S(1)} all-gather(f32[16,1,128]{2,0,1:T(8,128)} %bitcast.349), channel_id=1, replica_groups=mesh['bricks'=64,'slab'=4] {'bricks'}, dimensions={0}, use_global_device_ids=true | all-gather | bytes 532480 | tf_op jit(solution)/shard_map/all_gather | solution.py:104
  66.6 18.3 %all-gather.4.cloned.1.call-done = f32[1024,3,128]{2,0,1:T(8,128)} async-done(((f32[16,3,128]{2,0,1:T(8,128)}), f32[1024,3,128]{2,0,1:T(8,128)}) %all-gather.4.cloned.1.call-update) | async-done | bytes 1572880 | tf_op jit(solution)/shard_map/all_gather | solution.py:100
  89.1 24.3 %while.50 = (s32[]{:T(128)}, f32[9,16,1,128]{3,2,1,0:T(1,128)S(1)}, f32[9,16,1,128]{3,2,1,0:T(1,128)S(1)}, f32[9,16,3,128]{3,2,1,0:T(4,128)S(1)}, f32[9,16,3,128...) while((s32[]{:T(128)}, f32[9,16,1,128]{3,2,1,0:T(1,128)S(1)}, f32[9,16,1,128]{3,2,1,0:T(1,128)S(1)}, ...), condition=%wide.region_1.2_spmd, body=%wide.region_0.1_spmd.sunk | while | flops 6029314 | bytes 263893 | solution.py:49
  89.2 2.6 fusion.197
  91.9 2.6 fusion.197
  94.6 2.6 fusion.197
  97.3 2.6 fusion.197
  100.0 2.6 fusion.197
  102.7 2.6 fusion.197
  105.4 2.6 fusion.197
  108.1 2.6 fusion.197
  110.8 2.6 fusion.197
  114.3 18.7 %while.51 = (s32[]{:T(128)}, f32[9,16,128]{2,1,0:T(8,128)S(1)}, f32[9,16,3,128]{3,2,1,0:T(4,128)S(1)}, f32[9,16,3,128]{3,2,1,0:T(4,128)S(1)}, f32[9,16]{1,0:T(8,128)S(1)}, /*index=5*/f32[9,16,128]{2,1,0:T(8,128)S(1)}, s32[]{:T(128)}) while((s32[]{:T(128)}, f32[9,16,128]{2,1,0:T(8,128)S(1)}, f32[9,16,3,128]{3,2,1,0:T(4,128)S(1)}, ...), condition=%wide.region_3.4_spmd, body=%wide.region_2.3_spmd.sunk | while | flops 6029314 | bytes 295197 | solution.py:64
  134.4 137.2 %reduce-scatter.3.cloned.1.call-done = f32[16,128]{1,0:T(8,128)} async-done(((f32[1024,128]{1,0:T(8,128)}), f32[16,128]{1,0:T(8,128)}) %reduce-scatter.3.cloned.1.call-update) | async-done | bytes 8208 | tf_op jit(solution)/shard_map/reduce_scatter | solution.py:125
  272.3 48.6 %all-gather = f32[1024,128]{1,0:T(8,128)S(1)} all-gather(f32[16,128]{1,0:T(8,128)S(1)} %div.42), channel_id=2, replica_groups=mesh['bricks'=64,'slab'=4] {'bricks'}, dimensions={0}, use_global_device_ids=true | all-gather | bytes 532480 | tf_op jit(solution)/shard_map/all_gather | solution.py:104
  322.2 24.3 %while.52 = (s32[]{:T(128)}, f32[9,16,1,128]{3,2,1,0:T(1,128)S(1)}, f32[9,16,1,128]{3,2,1,0:T(1,128)S(1)}, f32[9,16,3,128]{3,2,1,0:T(4,128)S(1)}, f32[9,16,3,128...) while((s32[]{:T(128)}, f32[9,16,1,128]{3,2,1,0:T(1,128)S(1)}, f32[9,16,1,128]{3,2,1,0:T(1,128)S(1)}, ...), condition=%wide.region_6.7_spmd, body=%wide.region_5.6_spmd.sunk | while | flops 6029314 | bytes 263893 | solution.py:49
  322.3 2.6 fusion.209
  325.0 2.6 fusion.209
  327.7 2.6 fusion.209
  330.4 2.6 fusion.209
  333.1 2.6 fusion.209
  338.5 2.6 fusion.209
  347.4 18.7 %while.53 = (s32[]{:T(128)}, f32[9,16,128]{2,1,0:T(8,128)S(1)}, f32[9,16,3,128]{3,2,1,0:T(4,128)S(1)}, f32[9,16,3,128]{3,2,1,0:T(4,128)S(1)}, f32[9,16]{1,0:T(8,128)S(1)}, /*index=5*/f32[9,16,128]{2,1,0:T(8,128)S(1)}, s32[]{:T(128)}) while((s32[]{:T(128)}, f32[9,16,128]{2,1,0:T(8,128)S(1)}, f32[9,16,3,128]{3,2,1,0:T(4,128)S(1)}, ...), condition=%wide.region_8.9_spmd, body=%wide.region_7.8_spmd.sunk | while | flops 6029314 | bytes 295197 | solution.py:64
  367.5 138.0 %reduce-scatter.5.cloned.1.call-done = f32[16,128]{1,0:T(8,128)} async-done(((f32[1024,128]{1,0:T(8,128)}), f32[16,128]{1,0:T(8,128)}) %reduce-scatter.5.cloned.1.call-update) | async-done | bytes 8208 | tf_op jit(solution)/shard_map/reduce_scatter | solution.py:125
  507.6 76.2 %all-gather.6.cloned.1.call-done = f32[1024,4,128]{2,1,0:T(4,128)} async-done(((f32[16,4,128]{2,1,0:T(4,128)}), f32[1024,4,128]{2,1,0:T(4,128)}) %all-gather.6.cloned.1.call-update) | async-done | bytes 2097168 | tf_op jit(solution)/shard_map/all_gather | solution.py:104
  586.8 24.2 %while.54 = (s32[]{:T(128)}, f32[9,16,4,128]{3,2,1,0:T(4,128)S(1)}, f32[9,16,4,128]{3,2,1,0:T(4,128)S(1)}, f32[9,16,3,128]{3,1,2,0:T(8,128)S(1)}, f32[9,16,3,128...) while((s32[]{:T(128)}, f32[9,16,4,128]{3,2,1,0:T(4,128)S(1)}, f32[9,16,4,128]{3,2,1,0:T(4,128)S(1)}, ...), condition=%wide.region_11.12_spmd, body=%wide.region_10.11_spmd.sunk | while | flops 15466498 | bytes 313049 | solution.py:49
  594.9 2.6 fusion.219
  605.7 2.6 fusion.219
  611.6 5.8 scatter_custom_fusion
  619.1 4.5 collective-permute-start.2
  625.6 2.8 collective-permute-start
  630.7 3.1 collective-permute-done.1
  (323 shorter events, 92.7 us)
Async XLA Ops:
  7.2 59.3 %copy-start.7 = (s32[64,1]{0,1:T(1,128)S(1)}, s32[64,1]{0,1:T(1,128)}, u32[]{:S(2)}) copy-start(s32[64,1]{0,1:T(1,128)} %param.25) | copy-start | bytes 772
  7.2 77.7 %all-gather.4.cloned.1.call-start = ((), (), s32[]{:S(2)}) async-start(), calls=%async_computation.2 | async-start | bytes 1597440 | tf_op jit(solution)/shard_map/all_gather | solution.py:100
  7.9 263.7 %reduce-scatter.3.cloned.1.call-start = ((), (), s32[]{:S(2)}) async-start(), calls=%async_computation.3 | async-start | bytes 532480 | tf_op jit(solution)/shard_map/reduce_scatter | solution.py:125
  89.0 24.3 %copy-start.2 = (f32[1,2048]{1,0:T(1,128)S(1)}, f32[1,2048]{1,0:T(1,128)}, u32[]{:S(2)}) copy-start(f32[1,2048]{1,0:T(1,128)} %param.21) | copy-start | bytes 24580
  89.1 24.3 %copy-start.4 = (s32[1,144]{1,0:T(1,128)S(1)}, s32[1,144]{1,0:T(1,128)}, u32[]{:S(2)}) copy-start(s32[1,144]{1,0:T(1,128)} %param.26) | copy-start | bytes 1732
  114.3 18.7 %copy-start.5 = (s32[1,144]{1,0:T(1,128)S(1)}, s32[1,144]{1,0:T(1,128)}, u32[]{:S(2)}) copy-start(s32[1,144]{1,0:T(1,128)} %param.27) | copy-start | bytes 1732
  114.3 157.4 %copy-start.3 = (f32[1,2048]{1,0:T(1,128)S(1)}, f32[1,2048]{1,0:T(1,128)}, u32[]{:S(2)}) copy-start(f32[1,2048]{1,0:T(1,128)} %param.23) | copy-start | bytes 24580
  134.4 371.2 %reduce-scatter.5.cloned.1.call-start = ((), (), s32[]{:S(2)}) async-start(), calls=%async_computation.4 | async-start | bytes 532480 | tf_op jit(solution)/shard_map/reduce_scatter | solution.py:125
  347.4 159.5 %copy-start = (f32[1,3,2048]{2,0,1:T(1,128)S(1)}, f32[1,3,2048]{2,0,1:T(1,128)}, u32[]{:S(2)}) copy-start(f32[1,3,2048]{2,0,1:T(1,128)} %param.22) | copy-start | bytes 73732
  347.4 160.1 %copy-start.6 = (s32[1,2048]{1,0:T(1,128)S(1)}, s32[1,2048]{1,0:T(1,128)}, u32[]{:S(2)}) copy-start(s32[1,2048]{1,0:T(1,128)} %param.29) | copy-start | bytes 24580
  367.5 216.2 %all-gather.6.cloned.1.call-start = ((), (), s32[]{:S(2)}) async-start(), calls=%async_computation.5 | async-start | bytes 2129920 | tf_op jit(solution)/shard_map/all_gather | solution.py:104
  586.8 24.4 %copy-start.1 = (f32[1,3,2048]{2,0,1:T(1,128)S(1)}, f32[1,3,2048]{2,0,1:T(1,128)}, u32[]{:S(2)}) copy-start(f32[1,3,2048]{2,0,1:T(1,128)} %param.20) | copy-start | bytes 73732
  619.1 11.2 %collective-permute-start.2 = (f32[4,1,128]{2,1,0:T(1,128)S(1)}, f32[4,1,128]{2,1,0:T(1,128)S(1)}, u32[]{:S(2)}, u32[]{:S(2)}) collective-permute-start(f32[4,1,128]{2,1,0:T(1,128)S(1)} %get-tuple-element.398), channel_id=1, source_target_pairs={{4,0},{8,4},{12,8},{16,12},{20,16},{24,20},{28,24},{32,28},{36,32}... | collective-permute-start | bytes 6152 | tf_op jit(solution)/shard_map/ppermute | solution.py:21
  623.6 7.0 %collective-permute-start.3 = (f32[4,1,128]{2,1,0:T(1,128)S(1)}, f32[4,1,128]{2,1,0:T(1,128)S(1)}, u32[]{:S(2)}, u32[]{:S(2)}) collective-permute-start(f32[4,1,128]{2,1,0:T(1,128)S(1)} %get-tuple-element.399), channel_id=1, source_target_pairs={{0,4},{4,8},{8,12},{12,16},{16,20},{20,24},{24,28},{28,32},{32,36}... | collective-permute-start | bytes 6152 | tf_op jit(solution)/shard_map/ppermute | solution.py:18
  625.6 5.1 collective-permute-start
  628.3 5.5 collective-permute-start.1
Sparse Core Ops, SparseCore 0:
  10.6 74.3 all-gather.3
  134.5 137.1 reduce-scatter.2
  367.6 137.8 reduce-scatter.4
  508.2 75.5 all-gather.5
where the time goes:
time: 642 us; the launch traced here: 641 us
  waiting for transfers between devices  374 us (58%)
  matrix products  106 us (17%)
  blocking collectives  102 us (16%)
  local copies, waits for them, and re-layouts  24.4 us (4%)
  between operations  14.7 us (2%)
  starting transfers between devices  10.7 us (2%)
  other arithmetic  7.51 us (1%)
    reduce_scatter x2, waiting for transfers between devices, on_device(): lax.psum_scatter(dense_sums.reshape(brick_count * cell_tiles, tile_width)...  275 us
    all_gather x2, blocking collectives, fetch_duals(): return lax.all_gather(values, 'bricks', axis=0, tiled=True)[wanted]  102 us
    all_gather x1, waiting for transfers between devices, fetch_duals(): return lax.all_gather(values, 'bricks', axis=0, tiled=True)[wanted]  76.2 us
    dot_general x27, matrix products, row_one_group(): jnp.einsum('tij,tcj->tci', kernel, value_piece, precision=lax.Precision.H...  70 us
    dot_general x18, matrix products, column_one_group(): jnp.einsum('tij,ti->tj', kernel, scale_piece, precision=lax.Precision.HIG...  35 us
    all_gather x1, waiting for transfers between devices, on_device(): every_cell = lax.all_gather(own_cells, 'bricks', axis=0, tiled=True)  18.3 us
  transfers between devices with their start and end apart: 8, of which 6 were waited for; matrix products, arithmetic and copies ran while one was open for 1% of the time, Pallas kernels for 0%

commit v1 on v0

--- a/solution.py
+++ b/solution.py
@@ -1,3 +1,4 @@
+import functools
 import jax
 import jax.numpy as jnp
 from jax import lax
@@ -8,6 +9,28 @@
 LB = 4
 EPS = 0.05
 tile_group = 16
+
+
+def _view_zone(inputs, bus_axis):
+    h_now, before, res = (lax.axis_size(bus_axis), lax.axis_index(bus_axis), inputs.shape[0])
+    block_last, arr_out = (inputs, 1)
+    while arr_out < h_now:
+        block_last = jnp.concatenate(
+            [
+                block_last,
+                lax.ppermute(
+                    block_last,
+                    axis_name=bus_axis,
+                    perm=[(s, (s - arr_out) % h_now) for s in range(h_now)],
+                ),
+            ],
+            axis=0,
+        )
+        arr_out = 2 * arr_out
+    return jnp.roll(block_last, before * res, 0)
+
+
+define_plate_all = functools.partial(_view_zone, bus_axis="bricks")
 
 
 def with_halo(block, sides, width):
@@ -101,7 +124,7 @@
     slot_cells = every_cell[wanted]
 
     def fetch_duals(values):
-        return lax.all_gather(values, "bricks", axis=0, tiled=True)[wanted]
+        return define_plate_all(values)[wanted]
 
     part_rows = part_tiles[buckets]
     cell_rows = slot_cells[slot_ids]

time: 642 us -> 640 us (level)
  blocking collectives: 102 us -> 0 us
  starting transfers between devices: 10.7 us -> 73 us
  waiting for transfers between devices: 374 us -> 396 us
  local copies, waits for them, and re-layouts: 24.4 us -> 36.9 us
    all_gather x2 -> x0, blocking collectives: 102 us -> none  [fetch_duals(): return lax.all_gather(values, 'bricks', axis=0, tiled=True)[wanted]]
    all_gather x1 -> x0, waiting for transfers between devices: 76.2 us -> none  [fetch_duals(): return lax.all_gather(values, 'bricks', axis=0, tiled=True)[wanted]]
    ppermute x0 -> x18, waiting for transfers between devices: none -> 75.3 us  [_view_zone(): lax.ppermute(block_last, axis_name=bus_axis, perm=[(s, (s - arr_out) % h_...]
    ppermute x0 -> x18, starting transfers between devices: none -> 52.7 us  [_view_zone(): lax.ppermute(block_last, axis_name=bus_axis, perm=[(s, (s - arr_out) % h_...]
    all_gather x1, waiting for transfers between devices: 18.3 us -> 34.3 us  [on_device(): every_cell = lax.all_gather(own_cells, 'bricks', axis=0, tiled=True)]
    ppermute x2, starting transfers between devices: 7.29 us -> 16.9 us  [with_halo(): lax.ppermute(lax.slice_in_dim(block, 0, width, axis=dim), axis, backward)]
    unnamed x16 -> x36, local copies, waits for them, and re-layouts: 0.06 us -> 9.48 us
    reduce_scatter x2, waiting for transfers between devices: 275 us -> 282 us  [on_device(): lax.psum_scatter(dense_sums.reshape(brick_count * cell_tiles, tile_width)...]
  transfers between devices with their start and end apart: 8 -> 25, of which waited for: 6 -> 22; matrix products, arithmetic and copies ran while one was open for 1% -> 2% of each run, Pallas kernels for 0% -> 0%
where the time goes in v1:
time: 640 us
  waiting for transfers between devices  396 us (62%)
  matrix products  106 us (17%)
  starting transfers between devices  73 us (11%)
  local copies, waits for them, and re-layouts  36.9 us (6%)
  between operations  14.8 us (2%)
  other arithmetic  11 us (2%)
    reduce_scatter x2, waiting for transfers between devices, on_device(): lax.psum_scatter(dense_sums.reshape(brick_count * cell_tiles, tile_width)...  282 us
    ppermute x18, waiting for transfers between devices, _view_zone(): lax.ppermute(block_last, axis_name=bus_axis, perm=[(s, (s - arr_out) % h_...  75.3 us
    dot_general x27, matrix products, row_one_group(): jnp.einsum('tij,tcj->tci', kernel, value_piece, precision=lax.Precision.H...  70 us
    ppermute x18, starting transfers between devices, _view_zone(): lax.ppermute(block_last, axis_name=bus_axis, perm=[(s, (s - arr_out) % h_...  52.7 us
    dot_general x18, matrix products, column_one_group(): jnp.einsum('tij,ti->tj', kernel, scale_piece, precision=lax.Precision.HIG...  35 us
    all_gather x1, waiting for transfers between devices, on_device(): every_cell = lax.all_gather(own_cells, 'bricks', axis=0, tiled=True)  34.3 us
    ppermute x2, starting transfers between devices, with_halo(): lax.ppermute(lax.slice_in_dim(block, 0, width, axis=dim), axis, backward)  16.9 us
  transfers between devices with their start and end apart: 25, of which 22 were waited for; matrix products, arithmetic and copies ran while one was open for 2% of the time, Pallas kernels for 0%

profile of v1, /device:TPU:14, one launch (start us, length us, event | category | flops | bytes accessed | tf_op | source)
XLA Modules:
  0.0 639.5 jit_solution(7219246684619159528)
XLA Ops:
  8.6 5.3 collective-permute-start
  17.7 2.7 collective-permute-done.1
  22.6 3.5 collective-permute-done.2
  28.8 6.3 collective-permute-done.3
  35.1 3.4 collective-permute-start.4
  41.1 3.0 collective-permute-start.5
  46.4 3.3 collective-permute-done.5
  51.3 34.3 %all-gather.2.cloned.1.call-done = f32[1024,3,128]{2,0,1:T(8,128)} async-done(((f32[16,3,128]{2,0,1:T(8,128)}), f32[1024,3,128]{2,0,1:T(8,128)}) %all-gather.2.cloned.1.call-update) | async-done | bytes 1572880 | tf_op jit(solution)/shard_map/all_gather | solution.py:123
  89.8 24.3 %while.50 = (s32[]{:T(128)}, f32[9,16,1,128]{3,2,1,0:T(1,128)S(1)}, f32[9,16,1,128]{3,2,1,0:T(1,128)S(1)}, f32[9,16,3,128]{3,2,1,0:T(4,128)S(1)}, f32[9,16,3,128...) while((s32[]{:T(128)}, f32[9,16,1,128]{3,2,1,0:T(1,128)S(1)}, f32[9,16,1,128]{3,2,1,0:T(1,128)S(1)}, ...), condition=%wide.region_1.3_spmd, body=%wide.region_0.2_spmd.sunk | while | flops 6029314 | bytes 263893 | solution.py:72
  115.0 18.7 %while.51 = (s32[]{:T(128)}, f32[9,16,128]{2,1,0:T(8,128)S(1)}, f32[9,16,3,128]{3,2,1,0:T(4,128)S(1)}, f32[9,16,3,128]{3,2,1,0:T(4,128)S(1)}, f32[9,16]{1,0:T(8,128)S(1)}, /*index=5*/f32[9,16,128]{2,1,0:T(8,128)S(1)}, s32[]{:T(128)}) while((s32[]{:T(128)}, f32[9,16,128]{2,1,0:T(8,128)S(1)}, f32[9,16,3,128]{3,2,1,0:T(4,128)S(1)}, ...), condition=%wide.region_3.5_spmd, body=%wide.region_2.4_spmd.sunk | while | flops 6029314 | bytes 295197 | solution.py:87
  135.1 137.3 %reduce-scatter.3.cloned.1.call-done = f32[16,128]{1,0:T(8,128)} async-done(((f32[1024,128]{1,0:T(8,128)}), f32[16,128]{1,0:T(8,128)}) %reduce-scatter.3.cloned.1.call-update) | async-done | bytes 8208 | tf_op jit(solution)/shard_map/reduce_scatter | solution.py:148
  283.5 5.1 collective-permute-start.9
  288.7 3.2 collective-permute-done.9
  294.1 2.8 collective-permute-done.10
  296.9 3.4 collective-permute-start.11
  300.3 5.0 collective-permute-done.11
  306.9 24.3 %while.52 = (s32[]{:T(128)}, f32[9,16,1,128]{3,2,1,0:T(1,128)S(1)}, f32[9,16,1,128]{3,2,1,0:T(1,128)S(1)}, f32[9,16,3,128]{3,2,1,0:T(4,128)S(1)}, f32[9,16,3,128...) while((s32[]{:T(128)}, f32[9,16,1,128]{3,2,1,0:T(1,128)S(1)}, f32[9,16,1,128]{3,2,1,0:T(1,128)S(1)}, ...), condition=%wide.region_6.8_spmd, body=%wide.region_5.7_spmd.sunk | while | flops 6029314 | bytes 263893 | solution.py:72
  332.1 18.7 %while.53 = (s32[]{:T(128)}, f32[9,16,128]{2,1,0:T(8,128)S(1)}, f32[9,16,3,128]{3,2,1,0:T(4,128)S(1)}, f32[9,16,3,128]{3,2,1,0:T(4,128)S(1)}, f32[9,16]{1,0:T(8,128)S(1)}, /*index=5*/f32[9,16,128]{2,1,0:T(8,128)S(1)}, s32[]{:T(128)}) while((s32[]{:T(128)}, f32[9,16,128]{2,1,0:T(8,128)S(1)}, f32[9,16,3,128]{3,2,1,0:T(4,128)S(1)}, ...), condition=%wide.region_8.10_spmd, body=%wide.region_7.9_spmd.sunk | while | flops 6029314 | bytes 295197 | solution.py:87
  352.2 145.1 %reduce-scatter.5.cloned.1.call-done = f32[16,128]{1,0:T(8,128)} async-done(((f32[1024,128]{1,0:T(8,128)}), f32[16,128]{1,0:T(8,128)}) %reduce-scatter.5.cloned.1.call-update) | async-done | bytes 8208 | tf_op jit(solution)/shard_map/reduce_scatter | solution.py:148
  500.9 2.8 collective-permute-start.13
  506.0 2.9 collective-permute-start.14
  509.5 4.6 collective-permute-done.14
  514.1 4.9 collective-permute-start.15
  521.0 6.5 %collective-permute-done.15 = f32[128,4,128]{2,1,0:T(4,128)S(1)} collective-permute-done((f32[128,4,128]{2,1,0:T(4,128)S(1)}, f32[128,4,128]{2,1,0:T(4,128)S(1)}, u32[]{:S(2)}, u32[]{:S(2)}) %collective-permute-start.15) | collective-permute-done | bytes 262176 | tf_op jit(solution)/shard_map/ppermute | solution.py:21
  528.5 8.0 %collective-permute-start.16 = (f32[256,4,128]{2,1,0:T(4,128)S(1)}, f32[256,4,128]{2,1,0:T(4,128)S(1)}, u32[]{:S(2)}, u32[]{:S(2)}) collective-permute-start(f32[256,4,128]{2,1,0:T(4,128)S(1)} %get-tuple-element.405), channel_id=1, source_target_pairs={{0,192},{4,196},{8,200},{12,204},{16,208},{20,212},{24,216},{28,22... | collective-permute-start | bytes 1572872 | tf_op jit(solution)/shard_map/ppermute | solution.py:21
  536.4 7.7 %collective-permute-done.16 = f32[256,4,128]{2,1,0:T(4,128)S(1)} collective-permute-done((f32[256,4,128]{2,1,0:T(4,128)S(1)}, f32[256,4,128]{2,1,0:T(4,128)S(1)}, u32[]{:S(2)}, u32[]{:S(2)}) %collective-permute-start.16) | collective-permute-done | bytes 524320 | tf_op jit(solution)/shard_map/ppermute | solution.py:21
  547.2 19.1 %collective-permute-done.17 = f32[512,4,128]{2,1,0:T(4,128)S(1)} collective-permute-done((f32[512,4,128]{2,1,0:T(4,128)}, f32[512,4,128]{2,1,0:T(4,128)S(1)}, u32[]{:S(2)}, u32[]{:S(2)}) %collective-permute-start.17) | collective-permute-done | bytes 1048608 | tf_op jit(solution)/shard_map/ppermute | solution.py:21
  575.6 24.2 %while.54 = (s32[]{:T(128)}, f32[9,16,4,128]{3,2,1,0:T(4,128)S(1)}, f32[9,16,4,128]{3,2,1,0:T(4,128)S(1)}, f32[9,16,3,128]{3,1,2,0:T(8,128)S(1)}, f32[9,16,3,128...) while((s32[]{:T(128)}, f32[9,16,4,128]{3,2,1,0:T(4,128)S(1)}, f32[9,16,4,128]{3,2,1,0:T(4,128)S(1)}, ...), condition=%wide.region_11.13_spmd, body=%wide.region_10.12_spmd.sunk | while | flops 15466498 | bytes 313049 | solution.py:72
  600.4 5.8 scatter_custom_fusion
  607.9 14.0 %collective-permute-start.20 = (f32[4,1,128]{2,1,0:T(1,128)S(1)}, f32[4,1,128]{2,1,0:T(1,128)S(1)}, u32[]{:S(2)}, u32[]{:S(2)}) collective-permute-start(f32[4,1,128]{2,1,0:T(1,128)S(1)} %get-tuple-element.441), channel_id=1, source_target_pairs={{4,0},{8,4},{12,8},{16,12},{20,16},{24,20},{28,24},{32,28},{36,32}... | collective-permute-start | bytes 6152 | tf_op jit(solution)/shard_map/ppermute | solution.py:44
  623.9 2.9 collective-permute-start.18
  629.0 3.3 collective-permute-done.19
  (392 shorter events, 176.5 us)
Async XLA Ops:
  7.2 78.4 %all-gather.2.cloned.1.call-start = ((), (), s32[]{:S(2)}) async-start(), calls=%async_computation.2 | async-start | bytes 1597440 | tf_op jit(solution)/shard_map/all_gather | solution.py:123
  8.6 263.9 %reduce-scatter.3.cloned.1.call-start = ((), (), s32[]{:S(2)}) async-start(), calls=%async_computation.3 | async-start | bytes 532480 | tf_op jit(solution)/shard_map/reduce_scatter | solution.py:148
  8.6 7.4 %collective-permute-start = (f32[16,1,128]{2,0,1:T(8,128)}, f32[16,1,128]{2,0,1:T(8,128)S(1)}, u32[]{:S(2)}, u32[]{:S(2)}) collective-permute-start(f32[16,1,128]{2,0,1:T(8,128)} %bitcast.341), channel_id=1, source_target_pairs={{0,252},{4,0},{8,4},{12,8},{16,12},{20,16},{24,20},{28,24},{32,28}... | collective-permute-start | bytes 24584 | tf_op jit(solution)/shard_map/ppermute | solution.py:21
  16.7 3.7 collective-permute-start.1
  21.2 5.0 collective-permute-start.2
  26.9 8.2 %collective-permute-start.3 = (f32[128,1,128]{2,0,1:T(8,128)S(1)}, f32[128,1,128]{2,0,1:T(8,128)S(1)}, u32[]{:S(2)}, u32[]{:S(2)}) collective-permute-start(f32[128,1,128]{2,0,1:T(8,128)S(1)} %pad_maximum_fusion.2), channel_id=1, source_target_pairs={{0,224},{4,228},{8,232},{12,236},{16,240},{20,244},{24,248},{28,25... | collective-permute-start | bytes 196616 | tf_op jit(solution)/shard_map/ppermute | solution.py:21
  35.1 6.0 collective-permute-start.4
  41.1 8.5 %collective-permute-start.5 = (f32[512,1,128]{2,0,1:T(8,128)S(1)}, f32[512,1,128]{2,0,1:T(8,128)S(1)}, u32[]{:S(2)}, u32[]{:S(2)}) collective-permute-start(f32[512,1,128]{2,0,1:T(8,128)S(1)} %get-tuple-element.411), channel_id=1, source_target_pairs={{0,128},{4,132},{8,136},{12,140},{16,144},{20,148},{24,152},{28,15... | collective-permute-start | bytes 786440 | tf_op jit(solution)/shard_map/ppermute | solution.py:21
  89.7 24.3 %copy-start.2 = (f32[1,2048]{1,0:T(1,128)S(1)}, f32[1,2048]{1,0:T(1,128)}, u32[]{:S(2)}) copy-start(f32[1,2048]{1,0:T(1,128)} %param.23) | copy-start | bytes 24580
  89.8 24.3 %copy-start.4 = (s32[1,144]{1,0:T(1,128)S(1)}, s32[1,144]{1,0:T(1,128)}, u32[]{:S(2)}) copy-start(s32[1,144]{1,0:T(1,128)} %param.28) | copy-start | bytes 1732
  115.0 18.7 %copy-start.5 = (s32[1,144]{1,0:T(1,128)S(1)}, s32[1,144]{1,0:T(1,128)}, u32[]{:S(2)}) copy-start(s32[1,144]{1,0:T(1,128)} %param.29) | copy-start | bytes 1732
  115.0 157.5 %copy-start.3 = (f32[1,2048]{1,0:T(1,128)S(1)}, f32[1,2048]{1,0:T(1,128)}, u32[]{:S(2)}) copy-start(f32[1,2048]{1,0:T(1,128)} %param.25) | copy-start | bytes 24580
  135.1 362.3 %reduce-scatter.5.cloned.1.call-start = ((), (), s32[]{:S(2)}) async-start(), calls=%async_computation.4 | async-start | bytes 532480 | tf_op jit(solution)/shard_map/reduce_scatter | solution.py:148
  273.1 1.4 collective-permute-start.6
  274.5 4.2 collective-permute-start.7
  278.7 4.8 collective-permute-start.8
  283.5 8.3 %collective-permute-start.9 = (f32[128,1,128]{2,0,1:T(8,128)S(1)}, f32[128,1,128]{2,0,1:T(8,128)S(1)}, u32[]{:S(2)}, u32[]{:S(2)}) collective-permute-start(f32[128,1,128]{2,0,1:T(8,128)S(1)} %pad_maximum_fusion.3), channel_id=1, source_target_pairs={{0,224},{4,228},{8,232},{12,236},{16,240},{20,244},{24,248},{28,25... | collective-permute-start | bytes 196616 | tf_op jit(solution)/shard_map/ppermute | solution.py:21
  291.8 5.0 collective-permute-start.10
  296.9 8.4 %collective-permute-start.11 = (f32[512,1,128]{2,0,1:T(8,128)S(1)}, f32[512,1,128]{2,0,1:T(8,128)S(1)}, u32[]{:S(2)}, u32[]{:S(2)}) collective-permute-start(f32[512,1,128]{2,0,1:T(8,128)S(1)} %get-tuple-element.409), channel_id=1, source_target_pairs={{0,128},{4,132},{8,136},{12,140},{16,144},{20,148},{24,152},{28,15... | collective-permute-start | bytes 786440 | tf_op jit(solution)/shard_map/ppermute | solution.py:21
  332.1 166.6 %copy-start = (f32[1,3,2048]{2,0,1:T(1,128)S(1)}, f32[1,3,2048]{2,0,1:T(1,128)}, u32[]{:S(2)}) copy-start(f32[1,3,2048]{2,0,1:T(1,128)} %param.24) | copy-start | bytes 73732
  350.8 196.4 %copy-start.6 = (s32[1,2048]{1,0:T(1,128)S(1)}, s32[1,2048]{1,0:T(1,128)}, u32[]{:S(2)}) copy-start(s32[1,2048]{1,0:T(1,128)} %param.31) | copy-start | bytes 24580
  499.3 1.6 collective-permute-start.12
  500.9 5.0 collective-permute-start.13
  506.0 8.1 %collective-permute-start.14 = (f32[64,4,128]{2,1,0:T(4,128)S(1)}, f32[64,4,128]{2,1,0:T(4,128)S(1)}, u32[]{:S(2)}, u32[]{:S(2)}) collective-permute-start(f32[64,4,128]{2,1,0:T(4,128)S(1)} %pad_maximum_fusion.1), channel_id=1, source_target_pairs={{0,240},{4,244},{8,248},{12,252},{16,0},{20,4},{24,8},{28,12},{32,... | collective-permute-start | bytes 393224 | tf_op jit(solution)/shard_map/ppermute | solution.py:21
  514.1 13.4 %collective-permute-start.15 = (f32[128,4,128]{2,1,0:T(4,128)S(1)}, f32[128,4,128]{2,1,0:T(4,128)S(1)}, u32[]{:S(2)}, u32[]{:S(2)}) collective-permute-start(f32[128,4,128]{2,1,0:T(4,128)S(1)} %pad_maximum_fusion), channel_id=1, source_target_pairs={{0,224},{4,228},{8,232},{12,236},{16,240},{20,244},{24,248},{28,25... | collective-permute-start | bytes 786440 | tf_op jit(solution)/shard_map/ppermute | solution.py:21
  528.5 15.7 %collective-permute-start.16 = (f32[256,4,128]{2,1,0:T(4,128)S(1)}, f32[256,4,128]{2,1,0:T(4,128)S(1)}, u32[]{:S(2)}, u32[]{:S(2)}) collective-permute-start(f32[256,4,128]{2,1,0:T(4,128)S(1)} %get-tuple-element.405), channel_id=1, source_target_pairs={{0,192},{4,196},{8,200},{12,204},{16,208},{20,212},{24,216},{28,22... | collective-permute-start | bytes 1572872 | tf_op jit(solution)/shard_map/ppermute | solution.py:21
  545.2 21.1 %collective-permute-start.17 = (f32[512,4,128]{2,1,0:T(4,128)}, f32[512,4,128]{2,1,0:T(4,128)S(1)}, u32[]{:S(2)}, u32[]{:S(2)}) collective-permute-start(f32[512,4,128]{2,1,0:T(4,128)} %get-tuple-element.401), channel_id=1, source_target_pairs={{0,128},{4,132},{8,136},{12,140},{16,144},{20,148},{24,152},{28,15... | collective-permute-start | bytes 3145736 | tf_op jit(solution)/shard_map/ppermute | solution.py:21
  575.6 24.4 %copy-start.1 = (f32[1,3,2048]{2,0,1:T(1,128)S(1)}, f32[1,3,2048]{2,0,1:T(1,128)}, u32[]{:S(2)}) copy-start(f32[1,3,2048]{2,0,1:T(1,128)} %param.22) | copy-start | bytes 73732
  607.9 20.8 %collective-permute-start.20 = (f32[4,1,128]{2,1,0:T(1,128)S(1)}, f32[4,1,128]{2,1,0:T(1,128)S(1)}, u32[]{:S(2)}, u32[]{:S(2)}) collective-permute-start(f32[4,1,128]{2,1,0:T(1,128)S(1)} %get-tuple-element.441), channel_id=1, source_target_pairs={{4,0},{8,4},{12,8},{16,12},{20,16},{24,20},{28,24},{32,28},{36,32}... | collective-permute-start | bytes 6152 | tf_op jit(solution)/shard_map/ppermute | solution.py:44
  622.0 7.0 %collective-permute-start.21 = (f32[4,1,128]{2,1,0:T(1,128)S(1)}, f32[4,1,128]{2,1,0:T(1,128)S(1)}, u32[]{:S(2)}, u32[]{:S(2)}) collective-permute-start(f32[4,1,128]{2,1,0:T(1,128)S(1)} %get-tuple-element.442), channel_id=1, source_target_pairs={{0,4},{4,8},{8,12},{12,16},{16,20},{20,24},{24,28},{28,32},{32,36}... | collective-permute-start | bytes 6152 | tf_op jit(solution)/shard_map/ppermute | solution.py:41
  623.9 5.1 collective-permute-start.18
  626.8 5.5 collective-permute-start.19
Sparse Core Ops, SparseCore 0:
  10.5 75.0 all-gather.1
  135.2 137.2 reduce-scatter.2
  352.3 144.9 reduce-scatter.4
